TPU v7x, 32 devices: a whole 2x2x4 slice. The times are simulated.
32 devices in a mesh: dp: 8 (over y, x, core), expert: 4 (over z).
Axes of the slice: x: 2, y: 2, z: 4, core: 2. Of those that a mesh axis runs over, the one named last changes fastest.
Arguments:
- tokens: bfloat16 [512, 2048], P(('dp', 'expert')), may hold values from -6 to 6
- out_grad: bfloat16 [512, 2048], P(('dp', 'expert')), may hold values from -6 to 6
- gate_weights: bfloat16 [512, 2], P(('dp', 'expert')), may hold values from 0.049804688 to 1
- expert_ids: int32 [512, 2], P(('dp', 'expert')), may hold values from 0 to 3, all different within a row; in each aligned block of 16 rows (0 to 15, 16 to 31, ...) at most 10 rows name the same one
- swapped: int32 [4], replicated, may hold values from 0 to 1, as said below
- up_weight: bfloat16 [4, 2048, 384], P('expert'), may hold values from -0.125 to 0.125
- down_weight: bfloat16 [4, 384, 2048], P('expert'), may hold values from -0.3125 to 0.3125
Outputs:
- layer_out: bfloat16 [512, 2048], P(('dp', 'expert'))
- token_grad: bfloat16 [512, 2048], P(('dp', 'expert'))
- up_grad: float32 [4, 2048, 384], P('expert', 'dp')
- down_grad: float32 [4, 384, 2048], P('expert', 'dp')
Inputs may be any that keep to these rules, and one draw needn't show every extreme that they name: swapped[s] equals swapped[(s + 2) mod 4]; swapped[0] is 1. `expert_ids`: A token's 2 experts differ; at most 10 of the tokens of one device name one expert, and that many in some device.
All inputs are finite; a program needn't handle non-finite values.
Results may differ from a plain program's by a relative error of at most 0.023.
Values may be sent and summed in bfloat16 or wider, within the bound.
A program may use at most 64 MiB of HBM per device.

v0:
```python
import jax
import jax.numpy as jnp
from jax import lax
from jax.sharding import PartitionSpec as P


def partner(block, axis, stride):
    count = lax.axis_size(axis)
    route = []
    for low in range(count):
        high = low | 1 << stride
        if high != low and high < count:
            route += [(low, high), (high, low)]
    return lax.ppermute(block, axis, route)


def on_device(tokens, out_grad, gate_weights, expert_ids, swapped, up_weight, down_weight):
    owners = lax.axis_size("expert")
    mine = lax.axis_index("expert")
    exp_dev = up_weight.shape[0]
    width = tokens.shape[1]
    tok = tokens.shape[0]
    top = expert_ids.shape[1]
    experts = owners * exp_dev
    cap = tok * top // experts + max(2, tok // 32)
    pair_bit = owners.bit_length() - 2
    own_flags = lax.dynamic_slice_in_dim(swapped, mine * exp_dev, exp_dev, 0) == 1
    slot_flags = own_flags[:, None, None]
    moved_up, moved_down = partner((up_weight, down_weight), "expert", pair_bit)
    up_used = jnp.where(slot_flags, moved_up, up_weight)
    down_used = jnp.where(slot_flags, moved_down, down_weight)
    flags = swapped[expert_ids]
    target = jnp.where(flags == 1, (expert_ids + experts // 2) % experts, expert_ids)
    flat = target.reshape(-1)
    onehot = (flat[:, None] == jnp.arange(experts, dtype=jnp.int32)[None, :]).astype(jnp.int32)
    before = jnp.cumsum(onehot, axis=0) - onehot
    place_in = jnp.sum(before * onehot, axis=1)
    slot_row = (flat * cap + place_in).reshape(tok, top)
    match = slot_row[None, :, :] == jnp.arange(experts * cap, dtype=jnp.int32)[:, None, None]
    spread = jnp.any(match, axis=2).astype(jnp.bfloat16)
    gate_slot = jnp.sum(
        jnp.where(match, gate_weights.astype(jnp.float32)[None], 0.0), axis=(1, 2)
    ).astype(jnp.bfloat16)
    x_send = jnp.dot(spread, tokens, preferred_element_type=jnp.float32).astype(jnp.bfloat16)
    og_send = jnp.dot(spread, out_grad, preferred_element_type=jnp.float32).astype(jnp.bfloat16)
    recv_x, recv_og, recv_gate = (
        lax.all_to_all(
            x_send.reshape(owners, exp_dev * cap, width),
            "expert",
            split_axis=0,
            concat_axis=0,
            tiled=True,
        ),
        lax.all_to_all(
            og_send.reshape(owners, exp_dev * cap, width),
            "expert",
            split_axis=0,
            concat_axis=0,
            tiled=True,
        ),
        lax.all_to_all(
            gate_slot.reshape(owners, exp_dev * cap),
            "expert",
            split_axis=0,
            concat_axis=0,
            tiled=True,
        ),
    )
    rows = owners * cap
    x_rows = (
        recv_x.reshape(owners, exp_dev, cap, width)
        .transpose(1, 0, 2, 3)
        .reshape(exp_dev, rows, width)
    )
    og_rows = (
        recv_og.reshape(owners, exp_dev, cap, width)
        .transpose(1, 0, 2, 3)
        .reshape(exp_dev, rows, width)
    )
    gate_rows = recv_gate.reshape(owners, exp_dev, cap).transpose(1, 0, 2).reshape(exp_dev, rows)
    hidden = jnp.einsum("erd,edf->erf", x_rows, up_used, preferred_element_type=jnp.float32)
    active = jax.nn.silu(hidden).astype(jnp.bfloat16)
    y_rows = jnp.einsum(
        "erf,efd->erd", active, down_used, preferred_element_type=jnp.float32
    ).astype(jnp.bfloat16)
    dy_rows = (gate_rows.astype(jnp.float32)[:, :, None] * og_rows.astype(jnp.float32)).astype(
        jnp.bfloat16
    )
    d_active = jnp.einsum("erd,efd->erf", dy_rows, down_used, preferred_element_type=jnp.float32)
    sigma = jax.nn.sigmoid(hidden)
    d_hidden = (d_active * sigma * (1.0 + hidden * (1.0 - sigma))).astype(jnp.bfloat16)
    dx_rows = jnp.einsum(
        "erf,edf->erd", d_hidden, up_used, preferred_element_type=jnp.float32
    ).astype(jnp.bfloat16)
    part_down = jnp.einsum(
        "erf,erd->efd", active, dy_rows, preferred_element_type=jnp.float32
    ).astype(jnp.bfloat16)
    part_up = jnp.einsum(
        "erd,erf->edf", x_rows, d_hidden, preferred_element_type=jnp.float32
    ).astype(jnp.bfloat16)

    def to_sources(block):
        return (
            block.reshape(exp_dev, owners, cap, width)
            .transpose(1, 0, 2, 3)
            .reshape(owners, exp_dev * cap, width)
        )

    back_y, back_dx = (
        lax.all_to_all(to_sources(y_rows), "expert", split_axis=0, concat_axis=0, tiled=True),
        lax.all_to_all(to_sources(dx_rows), "expert", split_axis=0, concat_axis=0, tiled=True),
    )
    index_flat = slot_row.reshape(-1)
    y_pick = jnp.take(back_y.reshape(experts * cap, width), index_flat, axis=0).reshape(
        tok, top, width
    )
    dx_pick = jnp.take(back_dx.reshape(experts * cap, width), index_flat, axis=0).reshape(
        tok, top, width
    )
    layer_out = jnp.sum(
        gate_weights.astype(jnp.float32)[:, :, None] * y_pick.astype(jnp.float32), axis=1
    ).astype(jnp.bfloat16)
    token_grad = jnp.sum(dx_pick.astype(jnp.float32), axis=1).astype(jnp.bfloat16)
    reduced_up, reduced_down = (
        lax.psum_scatter(part_up, "dp", scatter_dimension=1, tiled=True).astype(jnp.float32),
        lax.psum_scatter(part_down, "dp", scatter_dimension=1, tiled=True).astype(jnp.float32),
    )
    return (layer_out, token_grad, reduced_up, reduced_down)


def solution(mesh):
    in_specs = (
        P(("dp", "expert"), None),
        P(("dp", "expert"), None),
        P(("dp", "expert"), None),
        P(("dp", "expert"), None),
        P(),
        P("expert", None, None),
        P("expert", None, None),
    )
    out_specs = (
        P(("dp", "expert"), None),
        P(("dp", "expert"), None),
        P("expert", "dp", None),
        P("expert", "dp", None),
    )
    return jax.shard_map(
        on_device, mesh=mesh, in_specs=in_specs, out_specs=out_specs, check_vma=False
    )
```

profile of v0, /device:TPU:0, one launch (start us, length us, event | category | flops | bytes accessed | tf_op | source)
XLA Modules:
  0.0 267.5 jit_solution(7054974699079632035)
XLA Ops:
  7.2 4.1 %collective-permute-start = (bf16[1,2048,384]{2,1,0:T(8,128)(2,1)}, bf16[1,2048,384]{2,1,0:T(8,128)(2,1)S(1)}, u32[]{:S(2)}, u32[]{:S(2)}) collective-permute-start(bf16[1,2048,384]{2,1,0:T(8,128)(2,1)} %param.14), channel_id=1, source_target_pairs={{0,2},{2,0},{1,3},{3,1},{4,6},{6,4},{5,7},{7,5},{8,10},{10,8},{9,1... | collective-permute-start | bytes 4718600 | tf_op jit(solution)/shard_map/ppermute | solution.py:14
  11.4 0.8 copy.44
  12.1 0.7 broadcast_add_fusion
  12.8 0.7 broadcast_compare_fusion
  13.6 0.1 copy.42
  13.8 0.7 gather_fusion
  14.9 0.2 select_reduce_fusion.1
  15.2 0.1 select_reduce_fusion
  15.3 0.7 convert_element_type.171
  16.0 5.1 %all-to-all-start.2 = ((bf16[4,1,10]{2,1,0:T(2,128)(2,1)}), bf16[4,1,10]{2,1,0:T(2,128)(2,1)S(1)}, u32[]{:S(2)}, u32[]{:S(2)}) async-start(bf16[4,1,10]{2,1,0:T(2,128)(2,1)} %convert_element_type.171), calls=%async_computation.2 | async-start | bytes 4096 | tf_op jit(solution)/shard_map/all_to_all | solution.py:61
  21.2 0.2 convolution_convert_fusion.5
  21.5 0.8 reshape.181
  22.2 124.9 %all-to-all-done.2 = bf16[4,1,10]{2,1,0:T(2,128)(2,1)S(1)} async-done(((bf16[4,1,10]{2,1,0:T(2,128)(2,1)}), bf16[4,1,10]{2,1,0:T(2,128)(2,1)S(1)}, u32[]{:S(2)}, u32[]{:S(2)}) %all-to-all-start.2) | async-done | bytes 112 | tf_op jit(solution)/shard_map/all_to_all | solution.py:61
  147.2 4.8 %all-to-all-start = ((bf16[4,10,2048]{2,1,0:T(8,128)(2,1)}), bf16[4,10,2048]{2,1,0:T(8,128)(2,1)S(1)}, u32[]{:S(2)}, u32[]{:S(2)}) async-start(bf16[4,10,2048]{2,1,0:T(8,128)(2,1)} %reshape.181), calls=%async_computation | async-start | bytes 524288 | tf_op jit(solution)/shard_map/all_to_all | solution.py:47
  152.0 0.9 convolution_convert_fusion.3
  152.9 1.7 reshape.186
  154.6 6.5 %all-to-all-done = bf16[4,10,2048]{2,1,0:T(8,128)(2,1)S(1)} async-done(((bf16[4,10,2048]{2,1,0:T(8,128)(2,1)}), bf16[4,10,2048]{2,1,0:T(8,128)(2,1)S(1)}, u32[]{:S(2)}, u32[]{:S(2)}) %all-to-all-start) | async-done | bytes 163872 | tf_op jit(solution)/shard_map/all_to_all | solution.py:47
  161.1 0.7 copy-done.4
  161.8 3.4 %all-to-all-start.3 = ((bf16[4,10,2048]{2,1,0:T(8,128)(2,1)}), bf16[4,10,2048]{2,1,0:T(8,128)(2,1)S(1)}, u32[]{:S(2)}, u32[]{:S(2)}) async-start(bf16[4,10,2048]{2,1,0:T(8,128)(2,1)} %reshape.186), calls=%async_computation.3 | async-start | bytes 524288 | tf_op jit(solution)/shard_map/all_to_all | solution.py:54
  165.2 0.6 dynamic_slice.3
  166.6 1.7 reshape.182
  168.3 3.8 %all-to-all-done.3 = bf16[4,10,2048]{2,1,0:T(8,128)(2,1)S(1)} async-done(((bf16[4,10,2048]{2,1,0:T(8,128)(2,1)}), bf16[4,10,2048]{2,1,0:T(8,128)(2,1)S(1)}, u32[]{:S(2)}, u32[]{:S(2)}) %all-to-all-start.3) | async-done | bytes 163872 | tf_op jit(solution)/shard_map/all_to_all | solution.py:54
  172.1 0.8 reshape.191
  172.8 1.5 fusion.6
  174.4 2.0 fusion.14
  176.5 0.6 copy-done.6
  177.1 1.8 fusion
  178.9 0.8 reshape.192
  179.7 2.8 %fusion.1 = bf16[1,384,2048]{2,1,0:T(8,128)(2,1)} fusion(f32[40,2048]{1,0:T(8,128)} %reshape.192, f32[40]{0:T(128)S(1)} %reshape.190, f32[40,384]{1,0:T(8,128)S(1)} %fusion.6), kind=kOutput, calls=%fused_computation.6 | convolution fusion | flops 63941632 | bytes 1962144 | tf_op jit(solution)/shard_map/erf,erd->efd/dot_general | solution.py:95
  182.6 0.7 convolution_convert_fusion.2
  183.4 0.8 reshape_transpose_reshape.10
  184.1 3.4 %all-to-all-start.4 = ((bf16[4,10,2048]{2,1,0:T(8,128)(2,1)}), bf16[4,10,2048]{2,1,0:T(8,128)(2,1)S(1)}, u32[]{:S(2)}, u32[]{:S(2)}) async-start(bf16[4,10,2048]{2,1,0:T(8,128)(2,1)} %reshape_transpose_reshape.10), calls=%async_computation.4 | async-start | bytes 524288 | tf_op jit(solution)/shard_map/all_to_all | solution.py:111
  187.5 1.9 convolution_convert_fusion.4
  189.5 0.8 reshape_transpose_reshape.4
  190.2 4.0 %all-to-all-done.4 = bf16[4,10,2048]{2,1,0:T(8,128)(2,1)S(1)} async-done(((bf16[4,10,2048]{2,1,0:T(8,128)(2,1)}), bf16[4,10,2048]{2,1,0:T(8,128)(2,1)S(1)}, u32[]{:S(2)}, u32[]{:S(2)}) %all-to-all-start.4) | async-done | bytes 163872 | tf_op jit(solution)/shard_map/all_to_all | solution.py:111
  194.3 3.4 %all-to-all-start.1 = ((bf16[4,10,2048]{2,1,0:T(8,128)(2,1)}), bf16[4,10,2048]{2,1,0:T(8,128)(2,1)S(1)}, u32[]{:S(2)}, u32[]{:S(2)}) async-start(bf16[4,10,2048]{2,1,0:T(8,128)(2,1)} %reshape_transpose_reshape.4), calls=%async_computation.1 | async-start | bytes 524288 | tf_op jit(solution)/shard_map/all_to_all | solution.py:110
  197.8 0.7 gather_fusion.2
  198.5 6.0 %all-to-all-done.1 = bf16[4,10,2048]{2,1,0:T(8,128)(2,1)S(1)} async-done(((bf16[4,10,2048]{2,1,0:T(8,128)(2,1)}), bf16[4,10,2048]{2,1,0:T(8,128)(2,1)S(1)}, u32[]{:S(2)}, u32[]{:S(2)}) %all-to-all-start.1) | async-done | bytes 163872 | tf_op jit(solution)/shard_map/all_to_all | solution.py:110
  204.6 0.7 gather_fusion.1
  205.2 0.1 broadcast_select_fusion.6
  205.3 0.1 reshape.189
  205.5 0.1 reshape.188
  205.6 1.0 reduce_sum.45
  206.5 1.0 multiply_reduce_fusion
  207.6 9.6 %reduce-scatter.3.cloned.1.call-done = bf16[1,256,384]{2,1,0:T(8,128)(2,1)} async-done(((bf16[1,2048,384]{2,1,0:T(8,128)(2,1)}), bf16[1,256,384]{2,1,0:T(8,128)(2,1)}) %reduce-scatter.3.cloned.1.call-update) | async-done | bytes 196624 | tf_op jit(solution)/shard_map/reduce_scatter | solution.py:125
  217.2 1.7 convert_element_type.160
  218.9 40.1 %reduce-scatter.5.cloned.1.call-done = bf16[1,48,2048]{2,1,0:T(8,128)(2,1)} async-done(((bf16[1,384,2048]{2,1,0:T(8,128)(2,1)}), bf16[1,48,2048]{2,1,0:T(8,128)(2,1)}) %reduce-scatter.5.cloned.1.call-update) | async-done | bytes 196624 | tf_op jit(solution)/shard_map/reduce_scatter | solution.py:126
  259.0 1.7 convert_element_type.166
  (55 shorter events, 1.4 us)
Async XLA Ops:
  7.2 14.1 %copy-start = (bf16[16,2048]{1,0:T(8,128)(2,1)S(1)}, bf16[16,2048]{1,0:T(8,128)(2,1)}, u32[]{:S(2)}) copy-start(bf16[16,2048]{1,0:T(8,128)(2,1)} %param.9) | copy-start | bytes 196612
  7.2 6.6 %copy-start.1 = (s32[4]{0:T(128)S(1)}, s32[4]{0:T(128)}, u32[]{:S(2)}) copy-start(s32[4]{0:T(128)} %param.13) | copy-start | bytes 52
  7.2 165.6 %collective-permute-start = (bf16[1,2048,384]{2,1,0:T(8,128)(2,1)}, bf16[1,2048,384]{2,1,0:T(8,128)(2,1)S(1)}, u32[]{:S(2)}, u32[]{:S(2)}) collective-permute-start(bf16[1,2048,384]{2,1,0:T(8,128)(2,1)} %param.14), channel_id=1, source_target_pairs={{0,2},{2,0},{1,3},{3,1},{4,6},{6,4},{5,7},{7,5},{8,10},{10,8},{9,1... | collective-permute-start | bytes 4718600 | tf_op jit(solution)/shard_map/ppermute | solution.py:14
  11.3 163.1 %collective-permute-start.1 = (bf16[1,384,2048]{2,1,0:T(8,128)(2,1)}, bf16[1,384,2048]{2,1,0:T(8,128)(2,1)}, u32[]{:S(2)}, u32[]{:S(2)}) collective-permute-start(bf16[1,384,2048]{2,1,0:T(8,128)(2,1)} %param.15), channel_id=1, source_target_pairs={{0,2},{2,0},{1,3},{3,1},{4,6},{6,4},{5,7},{7,5},{8,10},{10,8},{9,1... | collective-permute-start | bytes 4718600 | tf_op jit(solution)/shard_map/ppermute | solution.py:14
  13.8 1.4 copy-start.11
  13.8 138.2 %copy-start.8 = (bf16[16,2048]{1,0:T(8,128)(2,1)S(1)}, bf16[16,2048]{1,0:T(8,128)(2,1)}, u32[]{:S(2)}) copy-start(bf16[16,2048]{1,0:T(8,128)(2,1)} %param.10) | copy-start | bytes 196612
  15.1 1.0 copy-start.9
  16.0 131.1 %all-to-all-start.2 = ((bf16[4,1,10]{2,1,0:T(2,128)(2,1)}), bf16[4,1,10]{2,1,0:T(2,128)(2,1)S(1)}, u32[]{:S(2)}, u32[]{:S(2)}) async-start(bf16[4,1,10]{2,1,0:T(2,128)(2,1)} %convert_element_type.171), calls=%async_computation.2 | async-start | bytes 4096 | tf_op jit(solution)/shard_map/all_to_all | solution.py:61
  21.5 151.4 %copy-start.2 = (bf16[1,2048,384]{2,1,0:T(8,128)(2,1)S(1)}, bf16[1,2048,384]{2,1,0:T(8,128)(2,1)}, u32[]{:S(2)}) copy-start(bf16[1,2048,384]{2,1,0:T(8,128)(2,1)} %param.14) | copy-start | bytes 4718596
  147.2 13.9 %all-to-all-start = ((bf16[4,10,2048]{2,1,0:T(8,128)(2,1)}), bf16[4,10,2048]{2,1,0:T(8,128)(2,1)S(1)}, u32[]{:S(2)}, u32[]{:S(2)}) async-start(bf16[4,10,2048]{2,1,0:T(8,128)(2,1)} %reshape.181), calls=%async_computation | async-start | bytes 524288 | tf_op jit(solution)/shard_map/all_to_all | solution.py:47
  161.1 0.7 copy-start.4
  161.8 10.3 %all-to-all-start.3 = ((bf16[4,10,2048]{2,1,0:T(8,128)(2,1)}), bf16[4,10,2048]{2,1,0:T(8,128)(2,1)S(1)}, u32[]{:S(2)}, u32[]{:S(2)}) async-start(bf16[4,10,2048]{2,1,0:T(8,128)(2,1)} %reshape.186), calls=%async_computation.3 | async-start | bytes 524288 | tf_op jit(solution)/shard_map/all_to_all | solution.py:54
  165.2 52.0 %reduce-scatter.3.cloned.1.call-start = ((), (), s32[]{:S(2)}) async-start(), calls=%async_computation.7 | async-start | bytes 1769472 | tf_op jit(solution)/shard_map/reduce_scatter | solution.py:125
  172.8 1.6 copy-start.5
  172.8 1.6 copy-start.13
  174.4 2.7 %copy-start.3 = (bf16[40,2048]{1,0:T(8,128)(2,1)S(1)}, bf16[40,2048]{1,0:T(8,128)(2,1)}, u32[]{:S(2)}) copy-start(bf16[40,2048]{1,0:T(8,128)(2,1)} %reshape.182) | copy-start | bytes 491524
  176.5 0.6 copy-start.6
  178.9 80.1 %reduce-scatter.5.cloned.1.call-start = ((), (), s32[]{:S(2)}) async-start(), calls=%async_computation.8 | async-start | bytes 1769472 | tf_op jit(solution)/shard_map/reduce_scatter | solution.py:126
  179.7 2.8 %copy-start.12 = (bf16[16,2]{0,1:T(2,128)(2,1)S(1)}, bf16[16,2]{0,1:T(2,128)(2,1)}, u32[]{:S(2)}) copy-start(bf16[16,2]{0,1:T(2,128)(2,1)} %param.11) | copy-start | bytes 196
  179.7 2.9 %copy-start.7 = (bf16[40,384]{1,0:T(8,128)(2,1)S(1)}, bf16[40,384]{1,0:T(8,128)(2,1)}, u32[]{:S(2)}) copy-start(bf16[40,384]{1,0:T(8,128)(2,1)} %copy-done.6) | copy-start | bytes 92164
  184.1 10.2 %all-to-all-start.4 = ((bf16[4,10,2048]{2,1,0:T(8,128)(2,1)}), bf16[4,10,2048]{2,1,0:T(8,128)(2,1)S(1)}, u32[]{:S(2)}, u32[]{:S(2)}) async-start(bf16[4,10,2048]{2,1,0:T(8,128)(2,1)} %reshape_transpose_reshape.10), calls=%async_computation.4 | async-start | bytes 524288 | tf_op jit(solution)/shard_map/all_to_all | solution.py:111
  187.5 10.2 %copy-start.10 = (s32[32]{0:T(128)S(1)}, s32[32]{0:T(128)}, u32[]{:S(2)}) copy-start(s32[32]{0:T(128)} %copy-done.9) | copy-start | bytes 388
  194.3 10.2 %all-to-all-start.1 = ((bf16[4,10,2048]{2,1,0:T(8,128)(2,1)}), bf16[4,10,2048]{2,1,0:T(8,128)(2,1)S(1)}, u32[]{:S(2)}, u32[]{:S(2)}) async-start(bf16[4,10,2048]{2,1,0:T(8,128)(2,1)} %reshape_transpose_reshape.4), calls=%async_computation.1 | async-start | bytes 524288 | tf_op jit(solution)/shard_map/all_to_all | solution.py:110
Sparse Core Ops, SparseCore 0:
  179.0 38.1 reduce-scatter.2
  220.5 38.4 reduce-scatter.4
where the time goes:
time: 268 us
  waiting for transfers between devices  195 us (73%)
  starting transfers between devices  24.4 us (9%)
  between operations  15 us (6%)
  local copies, waits for them, and re-layouts  13.8 us (5%)
  matrix products  11.9 us (4%)
  other arithmetic  7.41 us (3%)
    all_to_all x1, waiting for transfers between devices, on_device(): lax.all_to_all(gate_slot.reshape(owners, exp_dev * cap), 'expert', split_...  125 us
    reduce_scatter x1, waiting for transfers between devices, on_device(): lax.psum_scatter(part_down, 'dp', scatter_dimension=1, tiled=True)  40.1 us
    reduce_scatter x1, waiting for transfers between devices, on_device(): lax.psum_scatter(part_up, 'dp', scatter_dimension=1, tiled=True)  9.64 us
    all_to_all x1, waiting for transfers between devices, on_device(): lax.all_to_all(x_send.reshape(owners, exp_dev * cap, width), 'expert', sp...  6.5 us
    all_to_all x1, waiting for transfers between devices, on_device(): lax.all_to_all(to_sources(y_rows), 'expert', split_axis=0, concat_axis=0,...  6.02 us
  transfers between devices with their start and end apart: 9, of which 7 were waited for; matrix products, arithmetic and copies ran while one was open for 10% of the time, Pallas kernels for 0%

commit v1 on v0

v1 whole, which is shorter than its diff:
```python
import jax
import jax.numpy as jnp
from jax import lax
from jax.sharding import PartitionSpec as P

BF = jnp.bfloat16
F32 = jnp.float32


def on_device(tokens, out_grad, gate_weights, expert_ids, swapped, up_weight, down_weight):
    owners = lax.axis_size("expert")
    mine = lax.axis_index("expert")
    width = tokens.shape[1]
    lanes = jnp.arange(128, dtype=jnp.int32)
    hit = expert_ids[:, :, None] == lanes[None, None, :]
    gates = jnp.sum(jnp.where(hit, gate_weights.astype(F32)[:, :, None], 0.0), axis=1).astype(BF)
    packed = jnp.concatenate([tokens, out_grad, gates], axis=1)
    full = lax.all_gather(packed, "expert", axis=0, tiled=True)
    x, og, gates = full[:, :width], full[:, width : 2 * width], full[:, 2 * width :]
    gates = gates.astype(F32)
    flag = lax.dynamic_slice_in_dim(swapped, mine, 1, 0)[0] == 1
    held = jnp.where(flag, (mine + owners // 2) % owners, mine)

    def column(e):
        return jnp.sum(jnp.where(lanes[None, :] == e, gates, 0.0), axis=1, keepdims=True)

    gate = column(mine)
    up, down = up_weight[0], down_weight[0]
    dy = (gate * og.astype(F32)).astype(BF)
    hidden = jnp.dot(x, up, preferred_element_type=F32)
    d_active = lax.dot_general(dy, down, (((1,), (1,)), ((), ())), preferred_element_type=F32)
    sigma = jax.nn.sigmoid(hidden)
    active = jnp.where(gate > 0, hidden * sigma, 0.0).astype(BF)
    d_hidden = (d_active * sigma * (1.0 + hidden * (1.0 - sigma))).astype(BF)
    other = lax.ppermute(
        jnp.concatenate([active, d_hidden], axis=1),
        "expert",
        [(i, (i + owners // 2) % owners) for i in range(owners)],
    )
    y = jnp.dot(active, down, preferred_element_type=F32).astype(BF).astype(F32)
    dx = lax.dot_general(d_hidden, up, (((1,), (1,)), ((), ())), preferred_element_type=F32)
    back = jnp.concatenate([(gate * y).astype(BF), dx.astype(BF)], axis=1)
    back = lax.psum_scatter(back, "expert", scatter_dimension=0, tiled=True)
    fw = active.shape[1]
    act_h = jnp.where(flag, other[:, :fw], active)
    dh_h = jnp.where(flag, other[:, fw:], d_hidden)
    dy_h = (column(held) * og.astype(F32)).astype(BF)
    over = (((0,), (0,)), ((), ()))
    part_up = lax.dot_general(x, dh_h, over, preferred_element_type=F32).astype(BF)
    part_down = lax.dot_general(act_h, dy_h, over, preferred_element_type=F32).astype(BF)
    sum_up = lax.psum_scatter(part_up, "dp", scatter_dimension=0, tiled=True).astype(F32)
    sum_down = lax.psum_scatter(part_down, "dp", scatter_dimension=0, tiled=True).astype(F32)
    return back[:, :width], back[:, width:], sum_up[None], sum_down[None]


def solution(mesh):
    rows = P(("dp", "expert"), None)
    in_specs = (rows, rows, rows, rows, P(), P("expert", None, None), P("expert", None, None))
    out_specs = (rows, rows, P("expert", "dp", None), P("expert", "dp", None))
    return jax.shard_map(
        on_device, mesh=mesh, in_specs=in_specs, out_specs=out_specs, check_vma=False
    )
```

time: 268 us -> 146 us (0.54)
  waiting for transfers between devices: 195 us -> 97.7 us
  starting transfers between devices: 24.4 us -> 0.93 us
  blocking collectives: 0 us -> 17.5 us
  local copies, waits for them, and re-layouts: 13.8 us -> 2.89 us
  matrix products: 11.9 us -> 5.55 us
    all_to_all x5 -> x0, waiting for transfers between devices: 145 us -> none  [the longest x1 125 us: on_device(): lax.all_to_all(gate_slot.reshape(owners, exp_dev * cap), 'expert', split_...]
    reduce_scatter x2 -> x3, waiting for transfers between devices: 49.7 us -> 92.9 us  [the longest x1 40.1 us: on_device(): lax.psum_scatter(part_up, 'dp', scatter_dimension=0, tiled=True).astype(F32)]
    all_to_all x5 -> x0, starting transfers between devices: 20.2 us -> none  [the longest x1 5.13 us: on_device(): lax.all_to_all(gate_slot.reshape(owners, exp_dev * cap), 'expert', split_...]
    all_gather x0 -> x1, blocking collectives: none -> 17.5 us  [on_device(): full = lax.all_gather(packed, 'expert', axis=0, tiled=True)]
    dot_general x8 -> x6, matrix products: 11.9 us -> 5.55 us  [the longest x1 1.78 us: on_device(): lax.dot_general(act_h, dy_h, over, preferred_element_type=F32).astype(BF)]
    ppermute x2 -> x1, waiting for transfers between devices: 0.01 us -> 4.77 us  [on_device(): lax.ppermute(jnp.concatenate([active, d_hidden], axis=1), 'expert', [(i,...]
    broadcast_in_dim x0 -> x2, other arithmetic: none -> 3.4 us  [on_device(): return (back[:, :width], back[:, width:], sum_up[None], sum_down[None])]
    ppermute x2 -> x1, starting transfers between devices: 4.18 us -> 0.81 us  [on_device(): lax.ppermute(jnp.concatenate([active, d_hidden], axis=1), 'expert', [(i,...]
  transfers between devices with their start and end apart: 9 -> 4, of which waited for: 7 -> 4; matrix products, arithmetic and copies ran while one was open for 10% -> 5% of each run, Pallas kernels for 0% -> 0%
where the time goes in v1:
time: 146 us
  waiting for transfers between devices  97.7 us (67%)
  blocking collectives  17.5 us (12%)
  between operations  14.5 us (10%)
  other arithmetic  6.76 us (5%)
  matrix products  5.55 us (4%)
  local copies, waits for them, and re-layouts  2.89 us (2%)
    reduce_scatter x1, waiting for transfers between devices, on_device(): lax.psum_scatter(part_up, 'dp', scatter_dimension=0, tiled=True).astype(F32)  40.1 us
    reduce_scatter x1, waiting for transfers between devices, on_device(): lax.psum_scatter(part_down, 'dp', scatter_dimension=0, tiled=True)  38.5 us
    all_gather x1, blocking collectives, on_device(): full = lax.all_gather(packed, 'expert', axis=0, tiled=True)  17.5 us
    reduce_scatter x1, waiting for transfers between devices, on_device(): back = lax.psum_scatter(back, 'expert', scatter_dimension=0, tiled=True)  14.2 us
    ppermute x1, waiting for transfers between devices, on_device(): lax.ppermute(jnp.concatenate([active, d_hidden], axis=1), 'expert', [(i,...  4.77 us
    broadcast_in_dim x2, other arithmetic, on_device(): return (back[:, :width], back[:, width:], sum_up[None], sum_down[None])  3.4 us
  transfers between devices with their start and end apart: 4, of which 4 were waited for; matrix products, arithmetic and copies ran while one was open for 5% of the time, Pallas kernels for 0%

profile of v1, /device:TPU:0, one launch (start us, length us, event | category | flops | bytes accessed | tf_op | source)
XLA Modules:
  0.0 145.8 jit_solution(18337395478298540508)
XLA Ops:
  7.2 0.0 copy-start
  7.2 0.0 reduce-scatter.4.cloned.1.call-start
  7.2 1.3 dynamic_slice.3
  9.2 0.0 copy-start.1
  9.3 0.8 convert_element_type.45
  10.0 0.8 select_reduce_fusion
  10.8 0.9 pad_maximum_fusion.1
  11.7 17.5 %all_gather.3 = bf16[64,4224]{1,0:T(8,128)(2,1)S(1)} all-gather(bf16[16,4224]{1,0:T(8,128)(2,1)S(1)} %pad_maximum_fusion.1), channel_id=1, replica_groups=mesh['dp'=8,'expert'=4] {'expert'}, dimensions={0}, use_global_device_ids=true | all-gather | bytes 675840 | tf_op jit(solution)/shard_map/all_gather | solution.py:18
  29.2 0.1 fusion.31
  29.3 0.0 copy-done
  29.3 0.4 select_convert_fusion
  29.7 0.0 copy-done.1
  29.7 0.6 fusion.15
  30.3 0.4 fusion.2
  30.8 0.6 convolution_convert_fusion.2
  31.4 0.8 pad_maximum_fusion
  32.2 0.0 reduce-scatter.4.cloned.1.call-update
  32.2 0.0 reduce-scatter.8.cloned.1.call-start
  32.3 0.8 collective-permute-start
  33.1 4.8 %collective-permute-done = bf16[64,768]{1,0:T(8,128)(2,1)S(1)} collective-permute-done((bf16[64,768]{1,0:T(8,128)(2,1)S(1)}, bf16[64,768]{1,0:T(8,128)(2,1)S(1)}, u32[]{:S(2)}, u32[]{:S(2)}) %collective-permute-start) | collective-permute-done | bytes 98336 | tf_op jit(solution)/shard_map/ppermute | solution.py:35
  37.9 1.8 %convolution_convert_fusion = bf16[384,2048]{1,0:T(8,128)(2,1)} fusion(f32[64]{0:T(128)S(1)} %get-tuple-element.4, bf16[64,4224]{1,0:T(8,128)(2,1)S(1)} %all_gather.3, bf16[64,384]{1,0:T(8,128)(2,1)S(1)} %get-tuple-element.8, bf16[64,768]{1,0:T(8,128)(2,1)S(1)} %collective-permute-done, pred[]{:T(512)} %bitcast.2), kind=kOutput, calls=%fused_computation | convolution fusion | flops 101867520 | bytes 1933825 | tf_op jit(solution)/shard_map/dot_general | solution.py:50
  39.7 0.0 reduce-scatter.8.cloned.1.call-update
  39.7 0.0 reduce-scatter.6.cloned.1.call-start
  39.7 1.8 %convolution_convert_fusion.1 = bf16[2048,384]{1,0:T(8,128)(2,1)} fusion(bf16[64,4224]{1,0:T(8,128)(2,1)S(1)} %all_gather.3, bf16[64,384]{1,0:T(8,128)(2,1)S(1)} %fusion.15, bf16[64,768]{1,0:T(8,128)(2,1)S(1)} %collective-permute-done, pred[]{:T(512)} %bitcast.2), kind=kOutput, calls=%fused_computation.1 | convolution fusion | flops 101474304 | bytes 1933313 | tf_op jit(solution)/shard_map/dot_general | solution.py:49
  41.5 0.0 reduce-scatter.6.cloned.1.call-update
  41.5 14.2 %reduce-scatter.4.cloned.1.call-done = bf16[16,4096]{1,0:T(8,128)(2,1)} async-done(((bf16[64,4096]{1,0:T(8,128)(2,1)}), bf16[16,4096]{1,0:T(8,128)(2,1)}) %reduce-scatter.4.cloned.1.call-update) | async-done | bytes 131088 | tf_op jit(solution)/shard_map/reduce_scatter | solution.py:43
  55.8 1.5 %fusion.32 = (bf16[16,2048]{1,0:T(8,128)(2,1)}, bf16[16,2048]{1,0:T(8,128)(2,1)}) fusion(bf16[16,4096]{1,0:T(8,128)(2,1)} %reduce-scatter.4.cloned.1.call-done), kind=kLoop, calls=%fused_computation.46 | loop fusion | bytes 262144 | tf_op jit(solution)/shard_map/slice | solution.py:53
  57.3 38.5 %reduce-scatter.8.cloned.1.call-done = bf16[48,2048]{1,0:T(8,128)(2,1)} async-done(((bf16[384,2048]{1,0:T(8,128)(2,1)}), bf16[48,2048]{1,0:T(8,128)(2,1)}) %reduce-scatter.8.cloned.1.call-update) | async-done | bytes 196624 | tf_op jit(solution)/shard_map/reduce_scatter | solution.py:52
  95.8 1.7 %bitcast_convert_fusion = f32[1,48,2048]{2,1,0:T(8,128)} fusion(bf16[48,2048]{1,0:T(8,128)(2,1)} %reduce-scatter.8.cloned.1.call-done), kind=kLoop, calls=%fused_computation.27 | loop fusion | flops 98304 | bytes 589824 | tf_op jit(solution)/shard_map/broadcast_in_dim | solution.py:53
  97.5 40.1 %reduce-scatter.6.cloned.1.call-done = bf16[256,384]{1,0:T(8,128)(2,1)} async-done(((bf16[2048,384]{1,0:T(8,128)(2,1)}), bf16[256,384]{1,0:T(8,128)(2,1)}) %reduce-scatter.6.cloned.1.call-update) | async-done | bytes 196624 | tf_op jit(solution)/shard_map/reduce_scatter | solution.py:51
  137.6 1.7 %bitcast_convert_fusion.1 = f32[1,256,384]{2,1,0:T(8,128)} fusion(bf16[256,384]{1,0:T(8,128)(2,1)} %reduce-scatter.6.cloned.1.call-done), kind=kLoop, calls=%fused_computation.28 | loop fusion | flops 98304 | bytes 589824 | tf_op jit(solution)/shard_map/broadcast_in_dim | solution.py:53
  (3 shorter events, 0.0 us)
Async XLA Ops:
  7.2 22.2 %copy-start = (bf16[1,2048,384]{2,1,0:T(8,128)(2,1)S(1)}, bf16[1,2048,384]{2,1,0:T(8,128)(2,1)}, u32[]{:S(2)}) copy-start(bf16[1,2048,384]{2,1,0:T(8,128)(2,1)} %param.12) | copy-start | bytes 4718596
  7.2 48.6 %reduce-scatter.4.cloned.1.call-start = ((), (), s32[]{:S(2)}) async-start(), calls=%async_computation.3 | async-start | bytes 655360 | tf_op jit(solution)/shard_map/reduce_scatter | solution.py:43
  9.2 20.5 %copy-start.1 = (bf16[1,384,2048]{2,1,0:T(8,128)(2,1)S(1)}, bf16[1,384,2048]{2,1,0:T(8,128)(2,1)}, u32[]{:S(2)}) copy-start(bf16[1,384,2048]{2,1,0:T(8,128)(2,1)} %param.13) | copy-start | bytes 4718596
  32.2 63.6 %reduce-scatter.8.cloned.1.call-start = ((), (), s32[]{:S(2)}) async-start(), calls=%async_computation.5 | async-start | bytes 1769472 | tf_op jit(solution)/shard_map/reduce_scatter | solution.py:52
  32.3 5.6 %collective-permute-start = (bf16[64,768]{1,0:T(8,128)(2,1)S(1)}, bf16[64,768]{1,0:T(8,128)(2,1)S(1)}, u32[]{:S(2)}, u32[]{:S(2)}) collective-permute-start(bf16[64,768]{1,0:T(8,128)(2,1)S(1)} %pad_maximum_fusion.2), channel_id=1, source_target_pairs={{0,2},{1,3},{2,0},{3,1},{4,6},{5,7},{6,4},{7,5},{8,10},{9,11},{10,... | collective-permute-start | bytes 294920 | tf_op jit(solution)/shard_map/ppermute | solution.py:35
  39.7 97.9 %reduce-scatter.6.cloned.1.call-start = ((), (), s32[]{:S(2)}) async-start(), calls=%async_computation.4 | async-start | bytes 1769472 | tf_op jit(solution)/shard_map/reduce_scatter | solution.py:51
Sparse Core Ops, SparseCore 0:
  32.3 23.3 reduce-scatter.3
  59.1 36.7 reduce-scatter.7
  99.1 38.4 reduce-scatter.5

commit v2 on v1

--- a/solution.py
+++ b/solution.py
@@ -1,13 +1,17 @@
+import functools
+
 import jax
 import jax.numpy as jnp
 from jax import lax
+from jax.experimental import pallas as pl
+from jax.experimental.pallas import tpu as pltpu
 from jax.sharding import PartitionSpec as P
 
 BF = jnp.bfloat16
 F32 = jnp.float32
 
 
-def on_device(tokens, out_grad, gate_weights, expert_ids, swapped, up_weight, down_weight):
+def by_collectives(tokens, out_grad, gate_weights, expert_ids, swapped, up_weight, down_weight):
     owners = lax.axis_size("expert")
     mine = lax.axis_index("expert")
     width = tokens.shape[1]
@@ -53,7 +57,245 @@
     return back[:, :width], back[:, width:], sum_up[None], sum_down[None]
 
 
+NT = (((1,), (1,)), ((), ()))
+TN = (((0,), (0,)), ((), ()))
+
+
+def dot(a, b, dims=(((1,), (0,)), ((), ()))):
+    return lax.dot_general(a, b, dims, preferred_element_type=F32)
+
+
+def kernel(
+    groups,
+    owners,
+    swapped_ref,
+    tok_ref,
+    og_ref,
+    gate_ref,
+    ids_ref,
+    up_ref,
+    down_ref,
+    out_ref,
+    tgrad_ref,
+    ugrad_ref,
+    dgrad_ref,
+    rows,
+    chunk_out,
+    chunk_in,
+    own,
+    other,
+    picked,
+    back_out,
+    back_in,
+    down_out,
+    down_in,
+    rows_send,
+    rows_recv,
+    chunk_send,
+    chunk_recv,
+    swap_send,
+    swap_recv,
+    pick_send,
+    pick_recv,
+    back_send,
+    back_recv,
+    down_send,
+    down_recv,
+):
+    tok, width = tok_ref.shape
+    fw = up_ref.shape[2]
+    part = width // groups
+    depth = fw // groups
+    count = owners * tok
+    me = lax.axis_index("expert")
+    group = lax.axis_index("dp")
+    half = owners // 2
+
+    def z_peer(k):
+        return lax.rem(me + k, owners)
+
+    def dp_peer(k):
+        return lax.rem(group + k, groups)
+
+    def send(src, dst, s, r, **where):
+        return pltpu.make_async_remote_copy(
+            src_ref=src,
+            dst_ref=dst,
+            send_sem=s,
+            recv_sem=r,
+            device_id=where,
+            device_id_type=pl.DeviceIdType.MESH,
+        )
+
+    barrier = pltpu.get_barrier_semaphore()
+    for k in range(1, owners):
+        pl.semaphore_signal(
+            barrier, inc=1, device_id={"expert": z_peer(k)}, device_id_type=pl.DeviceIdType.MESH
+        )
+    for k in range(1, groups):
+        pl.semaphore_signal(
+            barrier, inc=1, device_id={"dp": dp_peer(k)}, device_id_type=pl.DeviceIdType.MESH
+        )
+    lanes = lax.broadcasted_iota(jnp.int32, (tok, 128), 1)
+    dense = jnp.zeros((tok, 128), F32)
+    for k in range(ids_ref.shape[1]):
+        hit = ids_ref[:, k : k + 1] == lanes
+        dense += jnp.where(hit, gate_ref[:, k : k + 1].astype(F32), 0.0)
+    rows[me, :, :width] = tok_ref[...]
+    rows[me, :, width : 2 * width] = og_ref[...]
+    rows[me, :, 2 * width :] = dense.astype(BF)
+    flag = swapped_ref[me]
+    held = jnp.where(flag == 1, lax.rem(me + half, owners), me)
+    pl.semaphore_wait(barrier, owners + groups - 2)
+
+    started = []
+
+    def start(copy):
+        copy.start()
+        started.append(copy)
+
+    order = sorted(range(1, owners), key=lambda k: -min(k, owners - k))
+    for k in order:
+        start(
+            send(rows.at[me], rows.at[me], rows_send.at[k], rows_recv.at[me], expert=z_peer(k))
+        )
+    for k in range(1, owners):
+        p = z_peer(k)
+        send(rows.at[me], rows.at[p], rows_send.at[k], rows_recv.at[p], expert=p).wait_recv()
+
+    x = rows[:, :, :width].reshape(count, width)
+    og = rows[:, :, width : 2 * width].reshape(count, width).astype(F32)
+    gates = rows[:, :, 2 * width :].reshape(count, 128).astype(F32)
+    lane = lax.broadcasted_iota(jnp.int32, (count, 128), 1)
+
+    def column(e):
+        return jnp.sum(jnp.where(lane == e, gates, 0.0), axis=1, keepdims=True)
+
+    gate = column(me)
+    dy_held = (column(held) * og).astype(BF)
+    for j in range(groups):
+        chunk_out[j, :, :part] = x[:, j * part : (j + 1) * part]
+        chunk_out[j, :, part:] = dy_held[:, j * part : (j + 1) * part]
+    for k in range(1, groups):
+        p = dp_peer(k)
+        start(send(chunk_out.at[p], chunk_in.at[group], chunk_send.at[k], chunk_recv.at[group], dp=p))
+    chunk_in[group] = chunk_out[group]
+
+    up, down = up_ref[0], down_ref[0]
+    dy = (gate * og).astype(BF)
+    hidden = dot(x, up)
+    d_active = dot(dy, down, NT)
+    sigma = 1.0 / (1.0 + jnp.exp(-hidden))
+    active = jnp.where(gate > 0, hidden * sigma, 0.0).astype(BF)
+    d_hidden = (d_active * sigma * (1.0 + hidden * (1.0 - sigma))).astype(BF)
+    own[:, :fw] = active
+    own[:, fw:] = d_hidden
+    swap = send(own, other, swap_send, swap_recv, expert=lax.rem(me + half, owners))
+    start(swap)
+    y = dot(active, down).astype(BF).astype(F32)
+    back_out[:, :, :width] = (gate * y).astype(BF).reshape(owners, tok, width)
+    dx = dot(d_hidden, up, NT).astype(BF)
+    back_out[:, :, width:] = dx.reshape(owners, tok, width)
+    for k in order:
+        p = z_peer(k)
+        start(send(back_out.at[p], back_in.at[me], back_send.at[k], back_recv.at[me], expert=p))
+
+    swap.wait_recv()
+    picked[group] = jnp.where(flag == 1, other[...], own[...])
+    for k in range(1, groups):
+        p = dp_peer(k)
+        start(send(picked.at[group], picked.at[group], pick_send.at[k], pick_recv.at[group], dp=p))
+    for k in range(1, groups):
+        p = dp_peer(k)
+        send(chunk_out.at[p], chunk_in.at[p], chunk_send.at[k], chunk_recv.at[p], dp=p).wait_recv()
+    for k in range(1, groups):
+        p = dp_peer(k)
+        send(picked.at[group], picked.at[p], pick_send.at[k], pick_recv.at[p], dp=p).wait_recv()
+
+    total = groups * count
+    act_all = picked[:, :, :fw].reshape(total, fw)
+    dy_all = chunk_in[:, :, part:].reshape(total, part)
+    down_out[...] = dot(act_all, dy_all, TN).astype(BF).reshape(groups, depth, part)
+    for k in range(1, groups):
+        p = dp_peer(k)
+        start(send(down_out.at[p], down_in.at[group], down_send.at[k], down_recv.at[group], dp=p))
+    down_in[group] = down_out[group]
+    dh_all = picked[:, :, fw:].reshape(total, fw)
+    x_all = chunk_in[:, :, :part].reshape(total, part)
+    ugrad_ref[0] = dot(x_all, dh_all, TN)
+
+    acc = back_out[me].astype(F32)
+    for k in range(1, owners):
+        p = z_peer(k)
+        send(back_out.at[p], back_in.at[p], back_send.at[k], back_recv.at[p], expert=p).wait_recv()
+        acc += back_in[p].astype(F32)
+    out_ref[...] = acc[:, :width].astype(BF)
+    tgrad_ref[...] = acc[:, width:].astype(BF)
+    for k in range(1, groups):
+        p = dp_peer(k)
+        send(down_out.at[p], down_in.at[p], down_send.at[k], down_recv.at[p], dp=p).wait_recv()
+    for j in range(groups):
+        dgrad_ref[0, :, j * part : (j + 1) * part] = down_in[j].astype(F32)
+    for copy in started:
+        copy.wait_send()
+
+
+def by_kernel(groups, owners, tokens, out_grad, gate_weights, expert_ids, swapped, up, down):
+    tok, width = tokens.shape
+    fw = up.shape[2]
+    part, depth, count = width // groups, fw // groups, owners * tok
+    vmem = pl.BlockSpec(memory_space=pltpu.VMEM)
+    dma = pltpu.SemaphoreType.DMA
+    return pl.pallas_call(
+        functools.partial(kernel, groups, owners),
+        out_shape=(
+            jax.ShapeDtypeStruct((tok, width), BF),
+            jax.ShapeDtypeStruct((tok, width), BF),
+            jax.ShapeDtypeStruct((1, part, fw), F32),
+            jax.ShapeDtypeStruct((1, depth, width), F32),
+        ),
+        in_specs=[pl.BlockSpec(memory_space=pltpu.SMEM)] + [vmem] * 6,
+        out_specs=(vmem,) * 4,
+        scratch_shapes=[
+            pltpu.VMEM((owners, tok, 2 * width + 128), BF),
+            pltpu.VMEM((groups, count, 2 * part), BF),
+            pltpu.VMEM((groups, count, 2 * part), BF),
+            pltpu.VMEM((count, 2 * fw), BF),
+            pltpu.VMEM((count, 2 * fw), BF),
+            pltpu.VMEM((groups, count, 2 * fw), BF),
+            pltpu.VMEM((owners, tok, 2 * width), BF),
+            pltpu.VMEM((owners, tok, 2 * width), BF),
+            pltpu.VMEM((groups, depth, part), BF),
+            pltpu.VMEM((groups, depth, part), BF),
+            dma((owners,)),
+            dma((owners,)),
+            dma((groups,)),
+            dma((groups,)),
+            dma(()),
+            dma(()),
+            dma((groups,)),
+            dma((groups,)),
+            dma((owners,)),
+            dma((owners,)),
+            dma((groups,)),
+            dma((groups,)),
+        ],
+        compiler_params=pltpu.CompilerParams(
+            collective_id=0, has_side_effects=True, vmem_limit_bytes=48 << 20
+        ),
+    )(swapped, tokens, out_grad, gate_weights, expert_ids, up, down)
+
+
 def solution(mesh):
+    groups, owners = mesh.shape["dp"], mesh.shape["expert"]
+
+    def on_device(tokens, out_grad, gate_weights, expert_ids, swapped, up_weight, down_weight):
+        args = (tokens, out_grad, gate_weights, expert_ids, swapped, up_weight, down_weight)
+        width, fw = tokens.shape[1], up_weight.shape[2]
+        if width % (128 * groups) == 0 and fw % (16 * groups) == 0:
+            return by_kernel(groups, owners, *args)
+        return by_collectives(*args)
+
     rows = P(("dp", "expert"), None)
     in_specs = (rows, rows, rows, rows, P(), P("expert", None, None), P("expert", None, None))
     out_specs = (rows, rows, P("expert", "dp", None), P("expert", "dp", None))

time: 146 us -> 55.1 us (0.38)
  waiting for transfers between devices: 97.7 us -> 0 us
  Pallas kernels: 0 us -> 44.8 us
  blocking collectives: 17.5 us -> 0 us
  between operations: 14.5 us -> 0.65 us
  other arithmetic: 6.76 us -> 0 us
  local copies, waits for them, and re-layouts: 2.89 us -> 9.4 us
  matrix products: 5.55 us -> 0 us
    reduce_scatter x3 -> x0, waiting for transfers between devices: 92.9 us -> none  [the longest x1 40.1 us: on_device(): lax.psum_scatter(part_up, 'dp', scatter_dimension=0, tiled=True).astype(F32)]
    pallas_call x0 -> x1, Pallas kernels: none -> 44.8 us  [by_kernel(): pl.pallas_call(functools.partial(kernel, groups, owners), out_shape=(jax....]
    all_gather x1 -> x0, blocking collectives: 17.5 us -> none  [on_device(): full = lax.all_gather(packed, 'expert', axis=0, tiled=True)]
    unnamed x4 -> x16, local copies, waits for them, and re-layouts: 0.02 us -> 9.4 us
    dot_general x6 -> x0, matrix products: 5.55 us -> none  [the longest x1 1.78 us: on_device(): lax.dot_general(act_h, dy_h, over, preferred_element_type=F32).astype(BF)]
    ppermute x1 -> x0, waiting for transfers between devices: 4.77 us -> none  [on_device(): lax.ppermute(jnp.concatenate([active, d_hidden], axis=1), 'expert', [(i,...]
    broadcast_in_dim x2 -> x0, other arithmetic: 3.4 us -> none  [on_device(): return (back[:, :width], back[:, width:], sum_up[None], sum_down[None])]
    concatenate x3 -> x0, other arithmetic: 1.72 us -> none  [the longest x1 0.89 us: on_device(): packed = jnp.concatenate([tokens, out_grad, gates], axis=1)]
  transfers between devices with their start and end apart: 4 -> 0, of which waited for: 4 -> 0; matrix products, arithmetic and copies ran while one was open for 5% -> 0% of each run, Pallas kernels for 0% -> 0%
where the time goes in v2:
time: 55.1 us; the launch traced here: 54.8 us
  Pallas kernels  44.8 us (81%)
  local copies, waits for them, and re-layouts  9.4 us (17%)
  between operations  0.65 us (1%)
    pallas_call x1, Pallas kernels, by_kernel(): pl.pallas_call(functools.partial(kernel, groups, owners), out_shape=(jax....  44.8 us
    unnamed x16, local copies, waits for them, and re-layouts  9.4 us

profile of v2, /device:TPU:0, one launch (start us, length us, event | category | flops | bytes accessed | tf_op | source)
XLA Modules:
  0.0 54.8 jit_solution(11749180897734210939)
XLA Ops:
  0.6 0.7 %copy.11.gate_ref = bf16[16,2]{1,0:T(8,128)(2,1)S(1)} copy(bf16[16,2]{0,1:T(2,128)(2,1)} %param.9) | data formatting | bytes 128 | tf_op args[2]
  1.4 0.8 %copy.12.ids_ref = s32[16,2]{1,0:T(8,128)S(1)} copy(s32[16,2]{0,1:T(2,128)} %param.10) | data formatting | bytes 256 | tf_op args[3]
  2.1 0.0 copy-start
  2.1 1.4 %copy-done = bf16[1,2048,384]{2,1,0:T(8,128)(2,1)S(1)} copy-done((bf16[1,2048,384]{2,1,0:T(8,128)(2,1)S(1)}, bf16[1,2048,384]{2,1,0:T(8,128)(2,1)}, u32[]{:S(2)}) %copy-start) | copy-done | bytes 1572888
  3.5 0.0 copy-start.1
  3.5 1.4 %copy-done.1 = bf16[1,384,2048]{2,1,0:T(8,128)(2,1)S(1)} copy-done((bf16[1,384,2048]{2,1,0:T(8,128)(2,1)S(1)}, bf16[1,384,2048]{2,1,0:T(8,128)(2,1)}, u32[]{:S(2)}) %copy-start.1) | copy-done | bytes 1572888
  4.9 0.0 copy-start.2
  5.0 0.8 %copy-done.2 = bf16[16,2048]{1,0:T(8,128)(2,1)S(1)} copy-done((bf16[16,2048]{1,0:T(8,128)(2,1)S(1)}, bf16[16,2048]{1,0:T(8,128)(2,1)}, u32[]{:S(2)}) %copy-start.2) | copy-done | bytes 65560
  5.8 0.0 copy-start.3
  5.8 0.8 %copy-done.3 = bf16[16,2048]{1,0:T(8,128)(2,1)S(1)} copy-done((bf16[16,2048]{1,0:T(8,128)(2,1)S(1)}, bf16[16,2048]{1,0:T(8,128)(2,1)}, u32[]{:S(2)}) %copy-start.3) | copy-done | bytes 65560
  6.6 0.0 copy-start.4
  6.6 0.7 %copy-done.4 = s32[4]{0:T(128)S(1)} copy-done((s32[4]{0:T(128)S(1)}, s32[4]{0:T(128)}, u32[]{:S(2)}) %copy-start.4) | copy-done | bytes 40
  7.3 44.8 %shard_map.102 = (bf16[16,2048]{1,0:T(8,128)(2,1)S(1)}, bf16[16,2048]{1,0:T(8,128)(2,1)S(1)}, f32[1,256,384]{2,1,0:T(8,128)S(1)}, f32[1,48,2048]{2,1,0:T(8,128)S(1)}) custom-call(s32[4]{0:T(128)S(1)} %copy-done.4, bf16[16,2048]{1,0:T(8,128)(2,1)S(1)} %copy-done.2, bf16[16,2048]{1,0:T(8,128)(2,1)S(1)} %copy-done.3, bf16[16,2]{1,0:T(8,128)(2,1)S(1)} %copy.11.gate_ref, ...), custom_call_target="tpu_custom_call" | custom-call | tf_op jit(solution)/shard_map/pallas_call | solution.py:249
  52.1 0.6 %copy.17 = bf16[16,2048]{1,0:T(8,128)(2,1)} copy(bf16[16,2048]{1,0:T(8,128)(2,1)S(1)} %get-tuple-element.8) | data formatting | bytes 131072
  52.7 0.6 %copy.18 = bf16[16,2048]{1,0:T(8,128)(2,1)} copy(bf16[16,2048]{1,0:T(8,128)(2,1)S(1)} %get-tuple-element.9) | data formatting | bytes 131072
  53.3 0.7 %copy.19 = f32[1,256,384]{2,1,0:T(8,128)} copy(f32[1,256,384]{2,1,0:T(8,128)S(1)} %get-tuple-element.10) | data formatting | bytes 786432
  54.1 0.7 %copy.20 = f32[1,48,2048]{2,1,0:T(8,128)} copy(f32[1,48,2048]{2,1,0:T(8,128)S(1)} %get-tuple-element.11) | data formatting | bytes 786432
Async XLA Ops:
  2.1 1.4 %copy-start = (bf16[1,2048,384]{2,1,0:T(8,128)(2,1)S(1)}, bf16[1,2048,384]{2,1,0:T(8,128)(2,1)}, u32[]{:S(2)}) copy-start(bf16[1,2048,384]{2,1,0:T(8,128)(2,1)} %up_ref.1) | copy-start | bytes 4718596
  3.5 1.4 %copy-start.1 = (bf16[1,384,2048]{2,1,0:T(8,128)(2,1)S(1)}, bf16[1,384,2048]{2,1,0:T(8,128)(2,1)}, u32[]{:S(2)}) copy-start(bf16[1,384,2048]{2,1,0:T(8,128)(2,1)} %down_ref.1) | copy-start | bytes 4718596
  4.9 0.8 %copy-start.2 = (bf16[16,2048]{1,0:T(8,128)(2,1)S(1)}, bf16[16,2048]{1,0:T(8,128)(2,1)}, u32[]{:S(2)}) copy-start(bf16[16,2048]{1,0:T(8,128)(2,1)} %tok_ref.1) | copy-start | bytes 196612
  5.8 0.8 %copy-start.3 = (bf16[16,2048]{1,0:T(8,128)(2,1)S(1)}, bf16[16,2048]{1,0:T(8,128)(2,1)}, u32[]{:S(2)}) copy-start(bf16[16,2048]{1,0:T(8,128)(2,1)} %og_ref.1) | copy-start | bytes 196612
  6.6 0.7 %copy-start.4 = (s32[4]{0:T(128)S(1)}, s32[4]{0:T(128)}, u32[]{:S(2)}) copy-start(s32[4]{0:T(128)} %swapped_ref.1) | copy-start | bytes 52

commit v3 on v2

v3 whole, which is shorter than its diff:
```python
import functools

import jax
import jax.numpy as jnp
from jax import lax
from jax.experimental import pallas as pl
from jax.experimental.pallas import tpu as pltpu
from jax.sharding import PartitionSpec as P

BF = jnp.bfloat16
F32 = jnp.float32


def by_collectives(tokens, out_grad, gate_weights, expert_ids, swapped, up_weight, down_weight):
    owners = lax.axis_size("expert")
    mine = lax.axis_index("expert")
    width = tokens.shape[1]
    lanes = jnp.arange(128, dtype=jnp.int32)
    hit = expert_ids[:, :, None] == lanes[None, None, :]
    gates = jnp.sum(jnp.where(hit, gate_weights.astype(F32)[:, :, None], 0.0), axis=1).astype(BF)
    packed = jnp.concatenate([tokens, out_grad, gates], axis=1)
    full = lax.all_gather(packed, "expert", axis=0, tiled=True)
    x, og, gates = full[:, :width], full[:, width : 2 * width], full[:, 2 * width :]
    gates = gates.astype(F32)
    flag = lax.dynamic_slice_in_dim(swapped, mine, 1, 0)[0] == 1
    held = jnp.where(flag, (mine + owners // 2) % owners, mine)

    def column(e):
        return jnp.sum(jnp.where(lanes[None, :] == e, gates, 0.0), axis=1, keepdims=True)

    gate = column(mine)
    up, down = up_weight[0], down_weight[0]
    dy = (gate * og.astype(F32)).astype(BF)
    hidden = jnp.dot(x, up, preferred_element_type=F32)
    d_active = lax.dot_general(dy, down, (((1,), (1,)), ((), ())), preferred_element_type=F32)
    sigma = jax.nn.sigmoid(hidden)
    active = jnp.where(gate > 0, hidden * sigma, 0.0).astype(BF)
    d_hidden = (d_active * sigma * (1.0 + hidden * (1.0 - sigma))).astype(BF)
    other = lax.ppermute(
        jnp.concatenate([active, d_hidden], axis=1),
        "expert",
        [(i, (i + owners // 2) % owners) for i in range(owners)],
    )
    y = jnp.dot(active, down, preferred_element_type=F32).astype(BF).astype(F32)
    dx = lax.dot_general(d_hidden, up, (((1,), (1,)), ((), ())), preferred_element_type=F32)
    back = jnp.concatenate([(gate * y).astype(BF), dx.astype(BF)], axis=1)
    back = lax.psum_scatter(back, "expert", scatter_dimension=0, tiled=True)
    fw = active.shape[1]
    act_h = jnp.where(flag, other[:, :fw], active)
    dh_h = jnp.where(flag, other[:, fw:], d_hidden)
    dy_h = (column(held) * og.astype(F32)).astype(BF)
    over = (((0,), (0,)), ((), ()))
    part_up = lax.dot_general(x, dh_h, over, preferred_element_type=F32).astype(BF)
    part_down = lax.dot_general(act_h, dy_h, over, preferred_element_type=F32).astype(BF)
    sum_up = lax.psum_scatter(part_up, "dp", scatter_dimension=0, tiled=True).astype(F32)
    sum_down = lax.psum_scatter(part_down, "dp", scatter_dimension=0, tiled=True).astype(F32)
    return back[:, :width], back[:, width:], sum_up[None], sum_down[None]


NT = (((1,), (1,)), ((), ()))
TN = (((0,), (0,)), ((), ()))


def dot(a, b, dims=(((1,), (0,)), ((), ()))):
    return lax.dot_general(a, b, dims, preferred_element_type=F32)


def kernel(
    groups,
    owners,
    swapped_ref,
    tok_ref,
    og_ref,
    gate_ref,
    ids_ref,
    up_ref,
    down_ref,
    out_ref,
    tgrad_ref,
    ugrad_ref,
    dgrad_ref,
    xs,
    ogs,
    gs,
    up_buf,
    down_buf,
    dy_out,
    x_in,
    dy_in,
    own,
    other,
    picked,
    y_out,
    y_in,
    dx_out,
    dx_in,
    down_out,
    down_in,
    load,
    z_send,
    z_recv,
    dp_send,
    dp_recv,
    swap_send,
    swap_recv,
    pair_send,
    out_buf,
    tgrad_buf,
    ugrad_buf,
    dgrad_buf,
    store,
):
    tok, width = tok_ref.shape
    fw = up_ref.shape[2]
    part = width // groups
    depth = fw // groups
    count = owners * tok
    me = lax.axis_index("expert")
    group = lax.axis_index("dp")
    half = owners // 2
    twin = group + 1 - 2 * lax.rem(group, 2)

    def z_peer(k):
        return lax.rem(me + k, owners)

    def dp_peer(k):
        return lax.rem(group + k, groups)

    def cols(p):
        return pl.ds(pl.multiple_of(p * part, 128), part)

    def send(src, dst, s, r, **where):
        return pltpu.make_async_remote_copy(
            src_ref=src,
            dst_ref=dst,
            send_sem=s,
            recv_sem=r,
            device_id=where,
            device_id_type=pl.DeviceIdType.MESH,
        )

    barrier = pltpu.get_barrier_semaphore()
    for k in range(1, owners):
        pl.semaphore_signal(
            barrier, inc=1, device_id={"expert": z_peer(k)}, device_id_type=pl.DeviceIdType.MESH
        )
    for k in range(1, groups):
        pl.semaphore_signal(
            barrier, inc=1, device_id={"dp": dp_peer(k)}, device_id_type=pl.DeviceIdType.MESH
        )
    loads = [
        pltpu.make_async_copy(tok_ref, xs.at[me], load.at[0]),
        pltpu.make_async_copy(og_ref, ogs.at[me], load.at[1]),
        pltpu.make_async_copy(up_ref.at[0], up_buf, load.at[2]),
        pltpu.make_async_copy(down_ref.at[0], down_buf, load.at[3]),
    ]
    for copy in loads:
        copy.start()
    lines = lax.broadcasted_iota(jnp.int32, (128, tok), 0)
    dense = jnp.zeros((128, tok), F32)
    for k in range(ids_ref.shape[0]):
        hit = ids_ref[k : k + 1, :] == lines
        dense += jnp.where(hit, gate_ref[k : k + 1, :].astype(F32), 0.0)
    eye = (
        lax.broadcasted_iota(jnp.int32, (128, 128), 0)
        == lax.broadcasted_iota(jnp.int32, (128, 128), 1)
    ).astype(BF)
    gs[me] = dot(dense.astype(BF), eye, TN).astype(BF)
    flag = swapped_ref[me]
    held = jnp.where(flag == 1, lax.rem(me + half, owners), me)
    pl.semaphore_wait(barrier, owners + groups - 2)

    started = []

    def start(copy):
        copy.start()
        started.append(copy)

    order = sorted(range(1, owners), key=lambda k: -min(k, owners - k))
    blocks = ((tok_ref, xs), (gs.at[me], gs), (og_ref, ogs))
    for n, (src, dst) in enumerate(blocks):
        for k in order:
            start(
                send(src, dst.at[me], z_send.at[n, k], z_recv.at[n, me], expert=z_peer(k))
            )

    def arrive(n):
        for k in range(1, owners):
            p = z_peer(k)
            dst = blocks[n][1]
            send(dst.at[p], dst.at[p], z_send.at[n, k], z_recv.at[n, p], expert=p).wait_recv()

    loads[0].wait()
    arrive(0)
    for k in range(1, groups):
        p = dp_peer(k)
        start(
            send(xs.at[:, :, cols(p)], x_in.at[group], dp_send.at[0, k], dp_recv.at[0, group], dp=p)
        )
    x_in[group] = xs[:, :, cols(group)]
    loads[2].wait()
    up = up_buf[...]
    hidden = dot(xs[...].reshape(count, width), up)
    sigma = 1.0 / (1.0 + jnp.exp(-hidden))
    arrive(1)
    gates = gs[...].reshape(count, 128).astype(F32)
    lane = lax.broadcasted_iota(jnp.int32, (count, 128), 1)

    def column(e):
        return jnp.sum(jnp.where(lane == e, gates, 0.0), axis=1, keepdims=True)

    gate, gate_held = column(me), column(held)
    active = jnp.where(gate > 0, hidden * sigma, 0.0).astype(BF)
    own[:, :fw] = active
    loads[1].wait()
    loads[3].wait()
    down = down_buf[...]
    arrive(2)
    og = ogs[...].reshape(count, width).astype(F32)
    d_active = dot((gate * og).astype(BF), down, NT)
    d_hidden = (d_active * sigma * (1.0 + hidden * (1.0 - sigma))).astype(BF)
    own[:, fw:] = d_hidden
    swap = send(own, other, swap_send, swap_recv, expert=lax.rem(me + half, owners))
    start(swap)
    dy_out[...] = (gate_held * og).astype(BF).reshape(owners, tok, width)
    for k in range(1, groups):
        p = dp_peer(k)
        start(
            send(
                dy_out.at[:, :, cols(p)], dy_in.at[group], dp_send.at[1, k], dp_recv.at[1, group], dp=p
            )
        )
    dy_in[group] = dy_out[:, :, cols(group)]
    y = dot(active, down).astype(BF).astype(F32)
    y_out[...] = (gate * y).astype(BF).reshape(owners, tok, width)
    for k in order:
        p = z_peer(k)
        start(send(y_out.at[p], y_in.at[me], z_send.at[3, k], z_recv.at[3, me], expert=p))
    dx_out[...] = dot(d_hidden, up, NT).astype(BF).reshape(owners, tok, width)
    for k in order:
        p = z_peer(k)
        start(send(dx_out.at[p], dx_in.at[me], z_send.at[4, k], z_recv.at[4, me], expert=p))

    swap.wait_recv()
    picked[group] = jnp.where(flag == 1, other[...], own[...])
    mine = picked.at[group]
    for k in range(2, groups, 2):
        start(send(mine, mine, dp_send.at[2, k], dp_recv.at[2, group], dp=dp_peer(k)))
    start(send(mine, mine, dp_send.at[2, 0], dp_recv.at[2, group], dp=twin))
    for k in range(2, groups, 2):
        p = dp_peer(k)
        block = picked.at[p]
        send(block, block, dp_send.at[2, k], dp_recv.at[2, p], dp=p).wait_recv()
        start(send(block, block, pair_send.at[k], dp_recv.at[2, p], dp=twin))
    for n, dst in ((0, x_in), (1, dy_in)):
        for k in range(1, groups):
            p = dp_peer(k)
            send(dst.at[p], dst.at[p], dp_send.at[n, k], dp_recv.at[n, p], dp=p).wait_recv()
    for k in range(0, groups, 2):
        p = lax.rem(twin + k, groups)
        block = picked.at[p]
        send(block, block, dp_send.at[2, k], dp_recv.at[2, p], dp=twin).wait_recv()

    total = groups * count
    act_all = picked[:, :, :fw].reshape(total, fw)
    dy_all = dy_in[...].reshape(total, part)
    down_out[...] = dot(act_all, dy_all, TN).astype(BF).reshape(groups, depth, part)
    for k in range(1, groups):
        p = dp_peer(k)
        start(send(down_out.at[p], down_in.at[group], dp_send.at[3, k], dp_recv.at[3, group], dp=p))
    down_in[group] = down_out[group]
    dh_all = picked[:, :, fw:].reshape(total, fw)
    ugrad_buf[0] = dot(x_in[...].reshape(total, part), dh_all, TN)
    stores = [
        pltpu.make_async_copy(src, dst, store.at[i])
        for i, (src, dst) in enumerate(
            ((out_buf, out_ref), (tgrad_buf, tgrad_ref), (ugrad_buf, ugrad_ref), (dgrad_buf, dgrad_ref))
        )
    ]
    stores[2].start()

    for n, out, src, dst in ((3, out_buf, y_out, y_in), (4, tgrad_buf, dx_out, dx_in)):
        acc = src[me].astype(F32)
        for k in range(1, owners):
            p = z_peer(k)
            send(src.at[p], dst.at[p], z_send.at[n, k], z_recv.at[n, p], expert=p).wait_recv()
            acc += dst[p].astype(F32)
        out[...] = acc.astype(BF)
        stores[n - 3].start()
    for k in range(1, groups):
        p = dp_peer(k)
        send(down_out.at[p], down_in.at[p], dp_send.at[3, k], dp_recv.at[3, p], dp=p).wait_recv()
    for j in range(groups):
        dgrad_buf[0, :, j * part : (j + 1) * part] = down_in[j].astype(F32)
    stores[3].start()
    for copy in started:
        copy.wait_send()
    for copy in stores:
        copy.wait()


def place(*refs):
    count = (len(refs) - 1) // 2
    sems = refs[-1]
    copies = [
        pltpu.make_async_copy(refs[i], refs[count + i], sems.at[i]) for i in range(count)
    ]
    for copy in copies:
        copy.start()
    for copy in copies:
        copy.wait()


def by_kernel(groups, owners, tokens, out_grad, gate_weights, expert_ids, swapped, up, down):
    tok, width = tokens.shape
    fw = up.shape[2]
    part, depth, count = width // groups, fw // groups, owners * tok
    vmem = pl.BlockSpec(memory_space=pltpu.VMEM)
    hbm = pl.BlockSpec(memory_space=pltpu.HBM)
    dma = pltpu.SemaphoreType.DMA
    shapes = (
        jax.ShapeDtypeStruct((tok, width), BF),
        jax.ShapeDtypeStruct((tok, width), BF),
        jax.ShapeDtypeStruct((1, part, fw), F32),
        jax.ShapeDtypeStruct((1, depth, width), F32),
    )
    wide = pltpu.VMEM((owners, tok, width), BF)
    slim = pltpu.VMEM((groups, owners, tok, part), BF)
    hid = pltpu.VMEM((count, 2 * fw), BF)
    results = pl.pallas_call(
        functools.partial(kernel, groups, owners),
        out_shape=shapes,
        in_specs=[pl.BlockSpec(memory_space=pltpu.SMEM), hbm, hbm, vmem, vmem, hbm, hbm],
        out_specs=(hbm,) * 4,
        scratch_shapes=[
            wide,
            wide,
            pltpu.VMEM((owners, tok, 128), BF),
            pltpu.VMEM(up.shape[1:], BF),
            pltpu.VMEM(down.shape[1:], BF),
            wide,
            slim,
            slim,
            hid,
            hid,
            pltpu.VMEM((groups, count, 2 * fw), BF),
            wide,
            wide,
            wide,
            wide,
            pltpu.VMEM((groups, depth, part), BF),
            pltpu.VMEM((groups, depth, part), BF),
            dma((4,)),
            dma((5, owners)),
            dma((5, owners)),
            dma((4, groups)),
            dma((4, groups)),
            dma(()),
            dma(()),
            dma((groups,)),
            *[pltpu.VMEM(a.shape, a.dtype) for a in shapes],
            dma((4,)),
        ],
        compiler_params=pltpu.CompilerParams(
            collective_id=0, has_side_effects=True, vmem_limit_bytes=62 << 20
        ),
    )(swapped, tokens, out_grad, gate_weights.T, expert_ids.T, up, down)
    return pl.pallas_call(
        place,
        out_shape=shapes,
        in_specs=[pl.BlockSpec(memory_space=pl.ANY)] * 4,
        out_specs=(hbm,) * 4,
        scratch_shapes=[dma((4,))],
        compiler_params=pltpu.CompilerParams(vmem_limit_bytes=62 << 20),
    )(*results)


def solution(mesh):
    groups, owners = mesh.shape["dp"], mesh.shape["expert"]

    def on_device(tokens, out_grad, gate_weights, expert_ids, swapped, up_weight, down_weight):
        args = (tokens, out_grad, gate_weights, expert_ids, swapped, up_weight, down_weight)
        width, fw = tokens.shape[1], up_weight.shape[2]
        if width % (128 * groups) == 0 and fw % (16 * groups) == 0:
            return by_kernel(groups, owners, *args)
        return by_collectives(*args)

    rows = P(("dp", "expert"), None)
    in_specs = (rows, rows, rows, rows, P(), P("expert", None, None), P("expert", None, None))
    out_specs = (rows, rows, P("expert", "dp", None), P("expert", "dp", None))
    return jax.shard_map(
        on_device, mesh=mesh, in_specs=in_specs, out_specs=out_specs, check_vma=False
    )
```

time: 55.1 us -> 73 us (1.32)
  Pallas kernels: 44.8 us -> 72.2 us
  local copies, waits for them, and re-layouts: 9.4 us -> 0 us
    pallas_call x1 -> x2, Pallas kernels: 44.8 us -> 72.2 us  [the longest x1 43.3 us: by_kernel(): pl.pallas_call(functools.partial(kernel, groups, owners), out_shape=shape...]
    unnamed x16 -> x0, local copies, waits for them, and re-layouts: 9.4 us -> none
where the time goes in v3:
time: 73 us; the launch traced here: 72.8 us
  Pallas kernels  72.2 us (99%)
    pallas_call x1, Pallas kernels, by_kernel(): pl.pallas_call(functools.partial(kernel, groups, owners), out_shape=shape...  43.3 us
    pallas_call x1, Pallas kernels, by_kernel(): pl.pallas_call(place, out_shape=shapes, in_specs=[pl.BlockSpec(memory_spa...  28.9 us

profile of v3, /device:TPU:0, one launch (start us, length us, event | category | flops | bytes accessed | tf_op | source)
XLA Modules:
  0.0 72.8 jit_solution(2471920971290819089)
XLA Ops:
  0.6 43.3 %shard_map.102 = (bf16[16,2048]{1,0:T(8,128)(2,1)}, bf16[16,2048]{1,0:T(8,128)(2,1)}, f32[1,256,384]{2,1,0:T(8,128)}, f32[1,48,2048]{2,1,0:T(8,128)}) custom-call(s32[4]{0:T(128)} %swapped_ref.1, bf16[16,2048]{1,0:T(8,128)(2,1)} %tok_ref.1, bf16[16,2048]{1,0:T(8,128)(2,1)} %og_ref.1, bf16[2,16]{1,0:T(2,128)(2,1)} %bitcast.3, s32[2,16]{1,0:T(2,128)} %bitcast.2, ...), custom_call_target="tpu_custom_call" | custom-call | tf_op jit(solution)/shard_map/pallas_call | solution.py:330
  43.9 28.9 %shard_map.103 = (bf16[16,2048]{1,0:T(8,128)(2,1)}, bf16[16,2048]{1,0:T(8,128)(2,1)}, f32[1,256,384]{2,1,0:T(8,128)}, f32[1,48,2048]{2,1,0:T(8,128)}) custom-call(bf16[16,2048]{1,0:T(8,128)(2,1)} %get-tuple-element.8.refs_0_, bf16[16,2048]{1,0:T(8,128)(2,1)} %get-tuple-element.9.refs_1_, f32[1,256,384]{2,1,0:T(8,128)} %get-tuple-element.10.refs_2_, ...), custom_call_target="tpu_custom_call" | custom-call | tf_op jit(solution)/shard_map/pallas_call | solution.py:368

commit v4 on v3

--- a/solution.py
+++ b/solution.py
@@ -300,14 +300,17 @@
 
 
 def place(*refs):
-    count = (len(refs) - 1) // 2
-    sems = refs[-1]
-    copies = [
-        pltpu.make_async_copy(refs[i], refs[count + i], sems.at[i]) for i in range(count)
-    ]
-    for copy in copies:
+    count = (len(refs) - 2) // 3
+    loaded, stored = refs[-2:]
+    ins, outs, bufs = refs[:count], refs[count : 2 * count], refs[2 * count : 3 * count]
+    loads = [pltpu.make_async_copy(ins[i], bufs[i], loaded.at[i]) for i in range(count)]
+    stores = [pltpu.make_async_copy(bufs[i], outs[i], stored.at[i]) for i in range(count)]
+    for copy in loads:
         copy.start()
-    for copy in copies:
+    for load, store in zip(loads, stores):
+        load.wait()
+        store.start()
+    for copy in stores:
         copy.wait()
 
 
@@ -370,7 +373,7 @@
         out_shape=shapes,
         in_specs=[pl.BlockSpec(memory_space=pl.ANY)] * 4,
         out_specs=(hbm,) * 4,
-        scratch_shapes=[dma((4,))],
+        scratch_shapes=[pltpu.VMEM(a.shape, a.dtype) for a in shapes] + [dma((4,)), dma((4,))],
         compiler_params=pltpu.CompilerParams(vmem_limit_bytes=62 << 20),
     )(*results)
 

time: 73 us -> 46.1 us (0.63)
  Pallas kernels: 72.2 us -> 45.3 us
    pallas_call x1, Pallas kernels: 28.9 us -> 2.02 us  [by_kernel(): pl.pallas_call(place, out_shape=shapes, in_specs=[pl.BlockSpec(memory_spa...]
where the time goes in v4:
time: 46.1 us; the launch traced here: 45.9 us
  Pallas kernels  45.3 us (98%)
  between operations  0.64 us (1%)
    pallas_call x1, Pallas kernels, by_kernel(): pl.pallas_call(functools.partial(kernel, groups, owners), out_shape=shape...  43.3 us
    pallas_call x1, Pallas kernels, by_kernel(): pl.pallas_call(place, out_shape=shapes, in_specs=[pl.BlockSpec(memory_spa...  2.02 us

profile of v4, /device:TPU:0, one launch (start us, length us, event | category | flops | bytes accessed | tf_op | source)
XLA Modules:
  0.0 45.9 jit_solution(15370609378823491709)
XLA Ops:
  0.6 43.3 %shard_map.102 = (bf16[16,2048]{1,0:T(8,128)(2,1)}, bf16[16,2048]{1,0:T(8,128)(2,1)}, f32[1,256,384]{2,1,0:T(8,128)}, f32[1,48,2048]{2,1,0:T(8,128)}) custom-call(s32[4]{0:T(128)} %swapped_ref.1, bf16[16,2048]{1,0:T(8,128)(2,1)} %tok_ref.1, bf16[16,2048]{1,0:T(8,128)(2,1)} %og_ref.1, bf16[2,16]{1,0:T(2,128)(2,1)} %bitcast.3, s32[2,16]{1,0:T(2,128)} %bitcast.2, ...), custom_call_target="tpu_custom_call" | custom-call | tf_op jit(solution)/shard_map/pallas_call | solution.py:333
  43.9 2.0 %shard_map.103 = (bf16[16,2048]{1,0:T(8,128)(2,1)}, bf16[16,2048]{1,0:T(8,128)(2,1)}, f32[1,256,384]{2,1,0:T(8,128)}, f32[1,48,2048]{2,1,0:T(8,128)}) custom-call(bf16[16,2048]{1,0:T(8,128)(2,1)} %get-tuple-element.8.refs_0_, bf16[16,2048]{1,0:T(8,128)(2,1)} %get-tuple-element.9.refs_1_, f32[1,256,384]{2,1,0:T(8,128)} %get-tuple-element.10.refs_2_, ...), custom_call_target="tpu_custom_call" | custom-call | tf_op jit(solution)/shard_map/pallas_call | solution.py:371

commit v5 on v4

--- a/solution.py
+++ b/solution.py
@@ -109,6 +109,7 @@
     ugrad_buf,
     dgrad_buf,
     store,
+    line_send,
 ):
     tok, width = tok_ref.shape
     fw = up_ref.shape[2]
@@ -178,20 +179,50 @@
 
     order = sorted(range(1, owners), key=lambda k: -min(k, owners - k))
     blocks = ((tok_ref, xs), (gs.at[me], gs), (og_ref, ogs))
+    handed = []
+
+    def hand_on(n, src, b, cond, way):
+        copy = send(
+            src,
+            blocks[n][1].at[b],
+            line_send.at[way, n, b],
+            z_recv.at[n, b],
+            expert=lax.rem(me + owners + 1 - 2 * way, owners),
+        )
+
+        @pl.when(cond)
+        def _():
+            copy.start()
+
+        handed.append((cond, copy))
+
     for n, (src, dst) in enumerate(blocks):
-        for k in order:
-            start(
-                send(src, dst.at[me], z_send.at[n, k], z_recv.at[n, me], expert=z_peer(k))
-            )
-
-    def arrive(n):
-        for k in range(1, owners):
-            p = z_peer(k)
-            dst = blocks[n][1]
-            send(dst.at[p], dst.at[p], z_send.at[n, k], z_recv.at[n, p], expert=p).wait_recv()
-
+        hand_on(n, src, me, me < owners - 1, 0)
+        hand_on(n, src, me, me > 0, 1)
+
+    def arrive(n, d):
+        dst = blocks[n][1]
+        for way, there, on in (
+            (0, me >= d, me < owners - 1),
+            (1, me < owners - d, me > 0),
+        ):
+            b = lax.rem(me + owners - d if way == 0 else me + d, owners)
+
+            @pl.when(there)
+            def _():
+                send(
+                    dst.at[b], dst.at[b], line_send.at[way, n, b], z_recv.at[n, b], expert=b
+                ).wait_recv()
+
+            if d < owners - 1:
+                hand_on(n, dst.at[b], b, jnp.logical_and(there, on), way)
+
+    for d in range(1, owners - 1):
+        for n in range(3):
+            arrive(n, d)
+    last = owners - 1
     loads[0].wait()
-    arrive(0)
+    arrive(0, last)
     for k in range(1, groups):
         p = dp_peer(k)
         start(
@@ -202,7 +233,7 @@
     up = up_buf[...]
     hidden = dot(xs[...].reshape(count, width), up)
     sigma = 1.0 / (1.0 + jnp.exp(-hidden))
-    arrive(1)
+    arrive(1, last)
     gates = gs[...].reshape(count, 128).astype(F32)
     lane = lax.broadcasted_iota(jnp.int32, (count, 128), 1)
 
@@ -215,7 +246,7 @@
     loads[1].wait()
     loads[3].wait()
     down = down_buf[...]
-    arrive(2)
+    arrive(2, last)
     og = ogs[...].reshape(count, width).astype(F32)
     d_active = dot((gate * og).astype(BF), down, NT)
     d_hidden = (d_active * sigma * (1.0 + hidden * (1.0 - sigma))).astype(BF)
@@ -233,13 +264,7 @@
     dy_in[group] = dy_out[:, :, cols(group)]
     y = dot(active, down).astype(BF).astype(F32)
     y_out[...] = (gate * y).astype(BF).reshape(owners, tok, width)
-    for k in order:
-        p = z_peer(k)
-        start(send(y_out.at[p], y_in.at[me], z_send.at[3, k], z_recv.at[3, me], expert=p))
     dx_out[...] = dot(d_hidden, up, NT).astype(BF).reshape(owners, tok, width)
-    for k in order:
-        p = z_peer(k)
-        start(send(dx_out.at[p], dx_in.at[me], z_send.at[4, k], z_recv.at[4, me], expert=p))
 
     swap.wait_recv()
     picked[group] = jnp.where(flag == 1, other[...], own[...])
@@ -247,6 +272,12 @@
     for k in range(2, groups, 2):
         start(send(mine, mine, dp_send.at[2, k], dp_recv.at[2, group], dp=dp_peer(k)))
     start(send(mine, mine, dp_send.at[2, 0], dp_recv.at[2, group], dp=twin))
+    for k in order:
+        p = z_peer(k)
+        start(send(y_out.at[p], y_in.at[me], z_send.at[3, k], z_recv.at[3, me], expert=p))
+    for k in order:
+        p = z_peer(k)
+        start(send(dx_out.at[p], dx_in.at[me], z_send.at[4, k], z_recv.at[4, me], expert=p))
     for k in range(2, groups, 2):
         p = dp_peer(k)
         block = picked.at[p]
@@ -295,6 +326,12 @@
     stores[3].start()
     for copy in started:
         copy.wait_send()
+    for cond, copy in handed:
+
+        @pl.when(cond)
+        def _(copy=copy):
+            copy.wait_send()
+
     for copy in stores:
         copy.wait()
 
@@ -363,6 +400,7 @@
             dma((groups,)),
             *[pltpu.VMEM(a.shape, a.dtype) for a in shapes],
             dma((4,)),
+            dma((2, 3, owners)),
         ],
         compiler_params=pltpu.CompilerParams(
             collective_id=0, has_side_effects=True, vmem_limit_bytes=62 << 20

time: 46.1 us -> 39.5 us (0.86)
  Pallas kernels: 45.3 us -> 38.7 us
    pallas_call x1, Pallas kernels: 43.3 us -> 36.7 us  [by_kernel(): pl.pallas_call(functools.partial(kernel, groups, owners), out_shape=shape...]
where the time goes in v5:
time: 39.5 us; the launch traced here: 39.3 us
  Pallas kernels  38.7 us (98%)
  between operations  0.64 us (2%)
    pallas_call x1, Pallas kernels, by_kernel(): pl.pallas_call(functools.partial(kernel, groups, owners), out_shape=shape...  36.7 us
    pallas_call x1, Pallas kernels, by_kernel(): pl.pallas_call(place, out_shape=shapes, in_specs=[pl.BlockSpec(memory_spa...  2.02 us

profile of v5, /device:TPU:0, one launch (start us, length us, event | category | flops | bytes accessed | tf_op | source)
XLA Modules:
  0.0 39.3 jit_solution(17267978226044410312)
XLA Ops:
  0.6 36.7 %shard_map.102 = (bf16[16,2048]{1,0:T(8,128)(2,1)}, bf16[16,2048]{1,0:T(8,128)(2,1)}, f32[1,256,384]{2,1,0:T(8,128)}, f32[1,48,2048]{2,1,0:T(8,128)}) custom-call(s32[4]{0:T(128)} %swapped_ref.1, bf16[16,2048]{1,0:T(8,128)(2,1)} %tok_ref.1, bf16[16,2048]{1,0:T(8,128)(2,1)} %og_ref.1, bf16[2,16]{1,0:T(2,128)(2,1)} %bitcast.3, s32[2,16]{1,0:T(2,128)} %bitcast.2, ...), custom_call_target="tpu_custom_call" | custom-call | tf_op jit(solution)/shard_map/pallas_call | solution.py:370
  37.3 2.0 %shard_map.103 = (bf16[16,2048]{1,0:T(8,128)(2,1)}, bf16[16,2048]{1,0:T(8,128)(2,1)}, f32[1,256,384]{2,1,0:T(8,128)}, f32[1,48,2048]{2,1,0:T(8,128)}) custom-call(bf16[16,2048]{1,0:T(8,128)(2,1)} %get-tuple-element.8.refs_0_, bf16[16,2048]{1,0:T(8,128)(2,1)} %get-tuple-element.9.refs_1_, f32[1,256,384]{2,1,0:T(8,128)} %get-tuple-element.10.refs_2_, ...), custom_call_target="tpu_custom_call" | custom-call | tf_op jit(solution)/shard_map/pallas_call | solution.py:409
